TPU v7x, 32 devices: a whole 2x2x4 slice. The times are simulated.
32 devices in a mesh: chan: 8 (over y, x, core), tmpl: 4 (over z).
Axes of the slice: x: 2, y: 2, z: 4, core: 2. Of those that a mesh axis runs over, the one named last changes fastest.
Arguments:
- samples: bfloat16 [128, 384], P('chan'), may hold values from -200 to 200, as said below
- templates: bfloat16 [256, 16, 128], P('tmpl'), may hold values from -0.375 to 0.375
- start_chan: int32 [256], P('tmpl'), may hold values from 0 to 16, as said below
- chan_shift: int32 [128], P('chan'), may hold values from 0 to 128, as said below
- params: float32 [256, 16], P('tmpl'), may hold values from -4 to 4
Outputs:
- posterior: float32 [16, 128, 128], P(None, 'chan')
- evidence: float32 [128, 128], P('chan')
Inputs may be any that keep to these rules, and one draw needn't show every extreme that they name: `samples`: each channel's record carries an amplitude of its own. `start_chan`: both ends reached in every draw. `chan_shift`: both ends reached in every draw.
All inputs are finite; a program needn't handle non-finite values.
Results may differ from a plain program's by a relative error of at most 0.00125.
Values may be sent and summed in bfloat16 or wider, within the bound.
A program may use at most 128 MiB of HBM per device.

v0:
```python
import jax
import jax.numpy as jnp
from jax import lax
from jax.sharding import PartitionSpec as P

T_POS = 128
TCH = 16
TL = 128
PARAMS = 16
REACH = 16


def padded_2(cells, sides, width):
    for axis, dim in sides:
        count = lax.axis_size(axis)
        ends = count - 1
        head = lax.slice_in_dim(cells, 0, width, axis=dim)
        tail = lax.slice_in_dim(cells, cells.shape[dim] - width, cells.shape[dim], axis=dim)
        cells = jnp.concatenate(
            [
                lax.ppermute(tail, axis, [(i, (i + 1) % count) for i in range(ends)]),
                cells,
                lax.ppermute(head, axis, [((i + 1) % count, i) for i in range(ends)]),
            ],
            axis=dim,
        )
    return cells


def shifted_rows(samples, chan_shift):
    return jax.vmap(lambda row, s: lax.dynamic_slice_in_dim(row, s, T_POS + TL))(
        samples, chan_shift
    )


def make_patches(padded):
    return jnp.stack([padded[:, l : l + T_POS] for l in range(TL)], axis=-1).reshape(-1, TL)


def block_scores(patches, templates, start_chan, rows_out):
    rows_in = patches.shape[0] // T_POS
    count = templates.shape[0]
    flat = templates.reshape(count * TCH, TL)
    plane = lax.dot_general(
        flat, patches, (((1,), (1,)), ((), ())), preferred_element_type=jnp.float32
    )
    plane = plane.reshape(count, TCH, rows_in, T_POS)
    offsets = start_chan[:, None] + jnp.arange(TCH, dtype=jnp.int32)[None, :]
    pick_one = lambda r, s: lax.dynamic_slice_in_dim(r, s, rows_out, 0)
    picked = jax.vmap(jax.vmap(pick_one))(plane, offsets)
    return jnp.sum(picked, axis=1)


def body(samples, templates, start_chan, chan_shift, params):
    rows = samples.shape[0]
    aligned = shifted_rows(samples, chan_shift)
    padded = padded_2(aligned, (("chan", 0),), REACH)
    patches = make_patches(padded)
    scores = block_scores(patches, templates, start_chan, rows)
    count = scores.shape[0]
    local_top = jnp.max(scores, axis=0)
    weights = jnp.exp(scores - local_top[None])
    local_total = jnp.sum(weights, axis=0)
    numer = lax.dot_general(
        params,
        weights.reshape(count, rows * T_POS),
        (((0,), (0,)), ((), ())),
        precision=lax.Precision.HIGHEST,
        preferred_element_type=jnp.float32,
    )
    numer = numer.reshape(PARAMS, rows, T_POS)
    top = lax.pmax(local_top, "tmpl")
    factor = jnp.exp(local_top - top)
    total, summed = lax.psum((local_total * factor, numer * factor[None]), "tmpl")
    return (summed / total[None], top + jnp.log(total))


def solution(mesh):
    placed = (P("chan", None), P("tmpl", None, None), P("tmpl"), P("chan"), P("tmpl", None))
    return jax.shard_map(
        body,
        mesh=mesh,
        in_specs=placed,
        out_specs=(P(None, "chan", None), P("chan", None)),
        check_vma=False,
    )
```

profile of v0, /device:TPU:4, one launch (start us, length us, event | category | flops | bytes accessed | tf_op | source)
XLA Modules:
  0.0 256.0 jit_solution(11208844524643023641)
XLA Ops:
  7.2 0.7 fusion.7
  7.9 41.7 %while.1 = (s32[]{:T(128)}, bf16[16,384]{1,0:T(8,128)(2,1)}, s32[16,2]{0,1:T(2,128)S(1)}, bf16[16,256]{1,0:T(8,128)(2,1)S(1)}, s32[]{:T(128)}, /*index=5*/s32[]{:T(128)}) while((s32[]{:T(128)}, bf16[16,384]{1,0:T(8,128)(2,1)}, s32[16,2]{0,1:T(2,128)S(1)}, bf16[16,256]{1,0:T(8,128)(2,1)S(1)}, s32[]{:T(128)}, /*index=5*/s32[]{:T(128)}) %tuple.209), condition=%wide.while_cond, body=%wide.while_body.sunk | while | flops 2 | bytes 2161 | solution.py:31
  8.5 2.0 dynamic-slice.7
  11.2 2.0 dynamic-slice.7
  13.8 2.0 dynamic-slice.7
  16.4 2.0 dynamic-slice.7
  19.0 2.0 dynamic-slice.7
  21.6 2.0 dynamic-slice.7
  24.2 2.0 dynamic-slice.7
  26.8 2.0 dynamic-slice.7
  29.4 2.0 dynamic-slice.7
  32.0 2.0 dynamic-slice.7
  34.6 2.0 dynamic-slice.7
  37.2 2.0 dynamic-slice.7
  39.9 2.0 dynamic-slice.7
  42.5 2.0 dynamic-slice.7
  45.1 2.0 dynamic-slice.7
  47.7 2.0 dynamic-slice.7
  49.7 1.9 collective-permute-start
  51.6 4.5 %collective-permute-start.1 = (bf16[16,256]{1,0:T(8,128)(2,1)S(1)}, bf16[16,256]{1,0:T(8,128)(2,1)S(1)}, u32[]{:S(2)}, u32[]{:S(2)}) collective-permute-start(bf16[16,256]{1,0:T(8,128)(2,1)S(1)} %get-tuple-element.9), channel_id=1, source_target_pairs={{4,0},{8,4},{12,8},{16,12},{20,16},{24,20},{28,24},{5,1},{9,5},{13... | collective-permute-start | bytes 24584 | tf_op jit(solution)/shard_map/ppermute | solution.py:23
  56.2 0.7 fusion.6
  79.8 13.5 %stack.515 = bf16[6144,128]{0,1:T(8,128)(2,1)S(1)} concatenate(bf16[6144,1]{0,1:T(2,128)(2,1)} %get-tuple-element.163, bf16[6144,1]{0,1:T(2,128)(2,1)} %get-tuple-element.162, bf16[6144,1]{0,1:T(2,128)(2,1)} %get-tuple-element.161, bf16[6144,1]{0,1:T(2,128)(2,1)} %get-tuple-element.160, bf16[6144,1]{0,1:T(2,128)(2,1)} %get-tuple-element.159, bf16[6144,1]{0,1:T(2,128)(2,1)} %get-tuple-element.158, ...), dimensions={1} | concatenate | bytes 3145728 | tf_op jit(solution)/shard_map/stack | solution.py:37
  93.4 10.4 %convolution_bitcast_fusion = f32[1024,6144]{0,1:T(8,128)} fusion(bf16[6144,128]{0,1:T(8,128)(2,1)S(1)} %stack.515, bf16[1024,128]{1,0:T(8,128)(2,1)S(1)} %bitcast.804), kind=kOutput, calls=%fused_computation.2 | convolution fusion | flops 1610612736 | bytes 27000832 | tf_op jit(solution)/shard_map/dot_general | solution.py:44
  103.8 24.7 %copy.12 = f32[1024,6144]{1,0:T(8,128)} copy(f32[1024,6144]{0,1:T(8,128)} %convolution_bitcast_fusion) | data formatting | bytes 50331648 | tf_op jit(solution)/shard_map/dot_general | solution.py:44
  128.5 13.4 %copy.144 = f32[128,8,48,128]{3,2,1,0:T(8,128)S(1)} copy(f32[128,8,48,128]{3,1,2,0:T(8,128)} %bitcast.805) | data formatting | bytes 50331648
  141.9 15.1 %copy.13 = f32[64,16,48,128]{3,1,0,2:T(8,128)} copy(f32[64,16,48,128]{3,2,1,0:T(8,128)S(1)} %bitcast.806) | data formatting | bytes 50331648 | tf_op jit(solution)/shard_map/reshape | solution.py:47
  157.0 30.5 %gather_fusion = f32[1024,16,128]{2,0,1:T(8,128)} fusion(f32[64,16,48,128]{3,1,0,2:T(8,128)} %copy.13, s32[1024]{0:T(1024)S(1)} %reshape.339), kind=kCustom, calls=%fused_computation | custom fusion | bytes 16793600 | tf_op jit(solution)/shard_map/vmap(vmap())/gather | solution.py:49
  187.4 4.8 %bitcast_reduce_fusion = f32[64,16,128]{2,0,1:T(8,128)S(1)} fusion(f32[1024,16,128]{2,0,1:T(8,128)} %gather_fusion), kind=kLoop, calls=%fused_computation.3 | loop fusion | flops 1966080 | bytes 8912896 | tf_op jit(solution)/shard_map/reduce_sum | solution.py:51
  192.4 12.1 %pmax.7 = f32[16,128]{1,0:T(8,128)S(1)} all-reduce(f32[16,128]{1,0:T(8,128)S(1)} %reduce_max.9), channel_id=1, replica_groups=mesh['chan'=8,'tmpl'=4] {'tmpl'}, use_global_device_ids=true, to_apply=%region_2.0 | all-reduce | flops 2048 | bytes 16384 | tf_op jit(solution)/shard_map/pmax | solution.py:72
  204.5 8.5 %psum.15 = f32[16,128]{1,0:T(8,128)S(1)} all-reduce(f32[16,128]{1,0:T(8,128)S(1)} %get-tuple-element.18), channel_id=1, replica_groups=mesh['chan'=8,'tmpl'=4] {'tmpl'}, use_global_device_ids=true, to_apply=%region_5.0 | all-reduce | flops 2048 | bytes 16384 | tf_op jit(solution)/shard_map/psum | solution.py:74
  214.9 32.7 %all-reduce.3.cloned.1.call-done = f32[16,16,128]{2,1,0:T(8,128)} async-done(((f32[16,16,128]{2,1,0:T(8,128)}), f32[16,16,128]{2,1,0:T(8,128)}) %all-reduce.3.cloned.1.call-update) | async-done | bytes 131088 | tf_op jit(solution)/shard_map/psum | solution.py:74
  247.5 1.6 broadcast_divide_fusion
  (143 shorter events, 34.5 us)
Async XLA Ops:
  7.2 86.2 %copy-start = (bf16[64,16,128]{2,1,0:T(8,128)(2,1)S(1)}, bf16[64,16,128]{2,1,0:T(8,128)(2,1)}, u32[]{:S(2)}) copy-start(bf16[64,16,128]{2,1,0:T(8,128)(2,1)} %param.6) | copy-start | bytes 786436
  7.2 240.4 %all-reduce.3.cloned.1.call-start = ((), (), s32[]{:S(2)}) async-start(), calls=%async_computation | async-start | bytes 262144 | tf_op jit(solution)/shard_map/psum | solution.py:74
  49.7 7.3 %collective-permute-start = (bf16[16,256]{1,0:T(8,128)(2,1)S(1)}, bf16[16,256]{1,0:T(8,128)(2,1)S(1)}, u32[]{:S(2)}, u32[]{:S(2)}) collective-permute-start(bf16[16,256]{1,0:T(8,128)(2,1)S(1)} %get-tuple-element.9), channel_id=1, source_target_pairs={{0,4},{4,8},{8,12},{12,16},{16,20},{20,24},{24,28},{1,5},{5,9},{9,... | collective-permute-start | bytes 24584 | tf_op jit(solution)/shard_map/ppermute | solution.py:21
  51.6 5.9 %collective-permute-start.1 = (bf16[16,256]{1,0:T(8,128)(2,1)S(1)}, bf16[16,256]{1,0:T(8,128)(2,1)S(1)}, u32[]{:S(2)}, u32[]{:S(2)}) collective-permute-start(bf16[16,256]{1,0:T(8,128)(2,1)S(1)} %get-tuple-element.9), channel_id=1, source_target_pairs={{4,0},{8,4},{12,8},{16,12},{20,16},{24,20},{28,24},{5,1},{9,5},{13... | collective-permute-start | bytes 24584 | tf_op jit(solution)/shard_map/ppermute | solution.py:23
  157.0 92.1 %copy-start.1 = (bf16[64,16,128]{2,1,0:T(8,128)(2,1)S(1)}, bf16[64,16,128]{2,1,0:T(8,128)(2,1)}, u32[]{:S(2)}) copy-start(bf16[64,16,128]{2,1,0:T(8,128)(2,1)} %param.6) | copy-start | bytes 786436
  187.4 25.6 %copy-start.2 = (f32[64,16]{0,1:T(8,128)S(1)}, f32[64,16]{0,1:T(8,128)}, u32[]{:S(2)}) copy-start(f32[64,16]{0,1:T(8,128)} %param.9) | copy-start | bytes 12292
Sparse Core Ops, SparseCore 0:
  214.4 33.1 all-reduce.2
where the time goes:
time: 260 us; the launch traced here: 256 us
  local copies, waits for them, and re-layouts  161 us (62%)
  waiting for transfers between devices  33.2 us (13%)
  blocking collectives  20.6 us (8%)
  between operations  14.5 us (6%)
  matrix products  10.8 us (4%)
  other arithmetic  9.23 us (4%)
  starting transfers between devices  6.5 us (2%)
    gather x64, local copies, waits for them, and re-layouts  41.6 us
    another operation x65, local copies, waits for them, and re-layouts, make_patches(): jnp.stack([padded[:, l:l + T_POS] for l in range(TL)], axis=-1)  34.6 us
    psum x1, waiting for transfers between devices, body(): lax.psum((local_total * factor, numer * factor[None]), 'tmpl')  32.7 us
    gather x2, local copies, waits for them, and re-layouts, block_scores(): pick_one = lambda r, s: lax.dynamic_slice_in_dim(r, s, rows_out, 0)  30.6 us
    dot_general x1, local copies, waits for them, and re-layouts, block_scores(): lax.dot_general(flat, patches, (((1,), (1,)), ((), ())), preferred_elemen...  24.7 us
    reshape x1, local copies, waits for them, and re-layouts, block_scores(): plane = plane.reshape(count, TCH, rows_in, T_POS)  15.1 us
    unnamed x18, local copies, waits for them, and re-layouts  14.3 us
    pmax x1, blocking collectives, body(): top = lax.pmax(local_top, 'tmpl')  12.1 us
  transfers between devices with their start and end apart: 3, of which 2 were waited for; matrix products, arithmetic and copies ran while one was open for 1% of the time, Pallas kernels for 0%

commit v1 on v0

v1 whole, which is shorter than its diff:
```python
import functools

import jax
import jax.numpy as jnp
from jax import lax
from jax.experimental import pallas as pl
from jax.experimental.pallas import tpu as pltpu
from jax.sharding import PartitionSpec as P

T_POS = 128
TCH = 16
TL = 128
PARAMS = 16
REACH = 16
WIN = 2 * REACH
GROUP = 8
STEPS = 40
MESH = pl.DeviceIdType.MESH
F32, BF16 = jnp.float32, jnp.bfloat16


def column(row, n):
    wide = jnp.broadcast_to(row.astype(F32), (n, n))
    eye = lax.broadcasted_iota(jnp.int32, (n, n), 0) == lax.broadcasted_iota(jnp.int32, (n, n), 1)
    return jnp.sum(jnp.where(eye, wide, 0.0), axis=1, keepdims=True).astype(jnp.int32)


def build_filters(count, tmpl_ref, start_ref, tf, wp):
    tf[...] = tmpl_ref[...].astype(F32)
    start = column(start_ref[...], count)
    zero = jnp.zeros((count, (GROUP - 1) * TL), BF16)
    wp[:, : (GROUP - 1) * TL] = zero
    wp[:, (GROUP - 1 + WIN) * TL :] = jnp.zeros((count, GROUP * TL), BF16)
    step = 16
    for k0 in range(0, count, step):
        shift = jnp.broadcast_to(start[k0 : k0 + step], (step, TL))
        rows = [tf[pl.ds(k0 * TCH + j, step, stride=TCH), :] for j in range(TCH)]
        nothing = jnp.zeros((step, TL), F32)
        for bit in (1, 2, 4, 8, 16):
            on = (shift & bit) != 0
            size = min(WIN, len(rows) + bit)
            rows = [
                jnp.where(
                    on,
                    rows[r - bit] if r >= bit else nothing,
                    rows[r] if r < len(rows) else nothing,
                )
                for r in range(size)
            ]
        for r in range(WIN):
            wp[k0 : k0 + step, (GROUP - 1 + r) * TL : (GROUP + r) * TL] = rows[r].astype(BF16)


def build_hankel(block, first, e, h2):
    n = block.shape[0]
    for s in range(8):
        moved = block if s == 0 else pltpu.roll(block, 256 - s, 1)
        e[pl.ds(first * 8 + s, n, stride=8), :] = moved[:, :128]
        e[pl.ds((48 + first) * 8 + s, n, stride=8), :] = moved[:, 128:]
    lo = e[first * 8 : (first + n) * 8, :]
    hi = e[(48 + first) * 8 : (48 + first + n) * 8, :]
    both = jnp.concatenate([lo, hi], axis=1)

    def part(a):
        moved = both if a == 0 else pltpu.roll(both, 256 - 8 * a, 1)
        return moved[:, :128].reshape(n, 8, 128)

    for a in range(0, 16, 2):
        tile = jnp.concatenate([part(a), part(a + 1)], axis=1).astype(BF16)
        top = min(first + n, STEPS)
        if top > first:
            h2[first:top, 8 * a : 8 * a + 16, :128] = tile[: top - first]
        low = max(first, 8)
        h2[low - 8 : first + n - 8, 8 * a : 8 * a + 16, 128:] = tile[low - first :]


def kernel(
    nchan, nz, count,
    samples_ref, tmpl_ref, start_ref, shift_ref, params_ref,
    out_ref, ev_ref,
    al, halo, tf, wp, e, h2, comb, recv, gath,
    halo_send, halo_recv, rs_send, rs_recv, ag_send, ag_recv,
):
    cx, me = lax.axis_index("chan"), lax.axis_index("tmpl")
    q = 16 // nz
    has_left, has_right = cx > 0, cx < nchan - 1

    barrier = pltpu.get_barrier_semaphore()

    @pl.when(has_left)
    def _():
        pl.semaphore_signal(barrier, inc=1, device_id={"chan": cx - 1}, device_id_type=MESH)

    @pl.when(has_right)
    def _():
        pl.semaphore_signal(barrier, inc=1, device_id={"chan": cx + 1}, device_id_type=MESH)

    for d in range(1, nz):
        pl.semaphore_signal(
            barrier, inc=1, device_id={"tmpl": lax.rem(me + d, nz)}, device_id_type=MESH
        )

    x = samples_ref[...].astype(F32)
    shift = column(shift_ref[...], 16)
    for bit in (1, 2, 4, 8, 16, 32, 64, 128):
        on = (jnp.broadcast_to(shift, x.shape) & bit) != 0
        x = jnp.where(on, pltpu.roll(x, x.shape[1] - bit, 1), x)
    mine = x[:, : T_POS + TL]
    al[...] = mine.astype(BF16)

    pl.semaphore_wait(
        barrier, nz - 1 + has_left.astype(jnp.int32) + has_right.astype(jnp.int32)
    )

    def to_left():
        return pltpu.make_async_remote_copy(
            src_ref=al, dst_ref=halo.at[1], send_sem=halo_send.at[0], recv_sem=halo_recv.at[1],
            device_id={"chan": cx - 1}, device_id_type=MESH)

    def to_right():
        return pltpu.make_async_remote_copy(
            src_ref=al, dst_ref=halo.at[0], send_sem=halo_send.at[1], recv_sem=halo_recv.at[0],
            device_id={"chan": cx + 1}, device_id_type=MESH)

    @pl.when(has_left)
    def _():
        to_left().start()

    @pl.when(has_right)
    def _():
        to_right().start()

    build_filters(count, tmpl_ref, start_ref, tf, wp)
    build_hankel(mine, 16, e, h2)

    p = params_ref[...]
    p_hi = p.astype(BF16)
    p_lo = p - p_hi.astype(F32)
    below = (lax.broadcasted_iota(jnp.int32, (16, count), 0) == 0).astype(F32)
    pt_hi = jnp.concatenate([p_hi.astype(F32), below], axis=0).astype(BF16)
    pt_lo = jnp.concatenate([p_lo, jnp.zeros((16, count), F32)], axis=0).astype(BF16)

    @pl.when(has_left)
    def _():
        to_right().wait_recv()

    @pl.when(jnp.logical_not(has_left))
    def _():
        halo[0] = jnp.zeros((16, 256), BF16)

    @pl.when(has_right)
    def _():
        to_left().wait_recv()

    @pl.when(jnp.logical_not(has_right))
    def _():
        halo[1] = jnp.zeros((16, 256), BF16)

    build_hankel(halo[0].astype(F32), 0, e, h2)
    build_hankel(halo[1].astype(F32), 32, e, h2)

    lhs = jnp.concatenate(
        [wp[:, (GROUP - 1 - g) * TL : (GROUP - 1 - g + STEPS) * TL] for g in range(GROUP)], axis=0
    )
    scores = jnp.dot(lhs, h2[...].reshape(STEPS * TL, 256), preferred_element_type=F32)

    comb[:, q * 16 :, :] = jnp.zeros((nz, 8, 128), F32)

    def to_owner(z):
        slot = lax.rem(z - me + nz, nz)
        return pltpu.make_async_remote_copy(
            src_ref=comb.at[z], dst_ref=recv.at[slot], send_sem=rs_send.at[z],
            recv_sem=rs_recv.at[slot], device_id={"tmpl": z}, device_id_type=MESH)

    for g in range(GROUP):
        s = scores[g * count : (g + 1) * count]
        top = jnp.max(s, axis=0, keepdims=True)
        w = jnp.exp(s - top)
        w_hi = w.astype(BF16)
        w_lo = (w - w_hi.astype(F32)).astype(BF16)
        res = (
            jnp.dot(pt_hi, w_hi, preferred_element_type=F32)
            + jnp.dot(pt_hi, w_lo, preferred_element_type=F32)
            + jnp.dot(pt_lo, w_hi, preferred_element_type=F32)
        )
        total = res[PARAMS : PARAMS + 1]
        post = res[:PARAMS] / total
        ev = top + jnp.log(total)
        for half in range(2):
            i = 2 * g + half
            z, at = i // q, i % q
            comb[z, at * 16 : at * 16 + 16, :] = post[:, half * 128 : half * 128 + 128]
            comb[z, q * 16 + at : q * 16 + at + 1, :] = ev[:, half * 128 : half * 128 + 128]
            if at == q - 1:

                @pl.when(me != z)
                def _():
                    to_owner(z).start()

    for d in range(1, nz):
        pltpu.make_async_remote_copy(
            src_ref=comb.at[d], dst_ref=recv.at[d], send_sem=rs_send.at[d],
            recv_sem=rs_recv.at[d], device_id={"tmpl": lax.rem(me + d, nz)}, device_id_type=MESH
        ).wait_recv()

    evs = [comb[me, q * 16 :, :]] + [recv[d, q * 16 :, :] for d in range(1, nz)]
    top = functools.reduce(jnp.maximum, evs)
    parts = [jnp.exp(v - top) for v in evs]
    total = functools.reduce(jnp.add, parts)
    gath[me, q * 16 :, :] = top + jnp.log(total)
    inv = 1.0 / total
    shares = [v * inv for v in parts]
    for at in range(q):
        rows = slice(at * 16, at * 16 + 16)
        acc = shares[0][at : at + 1] * comb[me, rows, :]
        for d in range(1, nz):
            acc = acc + shares[d][at : at + 1] * recv[d, rows, :]
        gath[me, rows, :] = acc

    def to_peer(d):
        return pltpu.make_async_remote_copy(
            src_ref=gath.at[me], dst_ref=gath.at[me], send_sem=ag_send.at[d],
            recv_sem=ag_recv.at[me], device_id={"tmpl": lax.rem(me + d, nz)}, device_id_type=MESH)

    for d in range(1, nz):
        to_peer(d).start()
    for d in range(1, nz):
        z = lax.rem(me + d, nz)
        pltpu.make_async_remote_copy(
            src_ref=gath.at[z], dst_ref=gath.at[z], send_sem=ag_send.at[d],
            recv_sem=ag_recv.at[z], device_id={"tmpl": z}, device_id_type=MESH
        ).wait_recv()

    for i in range(16):
        c = 8 * (i % 2) + i // 2
        z, at = i // q, i % q
        out_ref[pl.ds(c, PARAMS, stride=16), :] = gath[z, at * 16 : at * 16 + 16, :]
        ev_ref[c : c + 1, :] = gath[z, q * 16 + at : q * 16 + at + 1, :]

    @pl.when(has_left)
    def _():
        to_left().wait_send()

    @pl.when(has_right)
    def _():
        to_right().wait_send()

    for z in range(nz):

        @pl.when(me != z)
        def _():
            to_owner(z).wait_send()

    for d in range(1, nz):
        to_peer(d).wait_send()


def solution(mesh):
    nchan, nz = mesh.shape["chan"], mesh.shape["tmpl"]

    def body(samples, templates, start_chan, chan_shift, params):
        rows, count = samples.shape[0], templates.shape[0]
        assert rows == 16 and 16 % nz == 0
        piece = 16 // nz * 16 + 8
        vmem = pl.BlockSpec(memory_space=pltpu.VMEM)
        dma = pltpu.SemaphoreType.DMA
        post, ev = pl.pallas_call(
            functools.partial(kernel, nchan, nz, count),
            out_shape=(
                jax.ShapeDtypeStruct((PARAMS * rows, T_POS), F32),
                jax.ShapeDtypeStruct((rows, T_POS), F32),
            ),
            in_specs=[vmem] * 5,
            out_specs=(vmem, vmem),
            scratch_shapes=[
                pltpu.VMEM((16, 256), BF16),
                pltpu.VMEM((2, 16, 256), BF16),
                pltpu.VMEM((count * TCH, TL), F32),
                pltpu.VMEM((count, (2 * GROUP - 1 + WIN) * TL), BF16),
                pltpu.VMEM((2 * 48 * 8, 128), F32),
                pltpu.VMEM((STEPS, TL, 256), BF16),
                pltpu.VMEM((nz, piece, 128), F32),
                pltpu.VMEM((nz, piece, 128), F32),
                pltpu.VMEM((nz, piece, 128), F32),
                dma((2,)),
                dma((2,)),
                dma((nz,)),
                dma((nz,)),
                dma((nz,)),
                dma((nz,)),
            ],
            compiler_params=pltpu.CompilerParams(
                collective_id=0, has_side_effects=True, vmem_limit_bytes=40 * 1024 * 1024
            ),
        )(
            samples,
            templates.reshape(count * TCH, TL),
            start_chan.reshape(1, count),
            chan_shift.reshape(1, rows),
            params.T,
        )
        return post.reshape(PARAMS, rows, T_POS), ev

    placed = (P("chan", None), P("tmpl", None, None), P("tmpl"), P("chan"), P("tmpl", None))
    return jax.shard_map(
        body,
        mesh=mesh,
        in_specs=placed,
        out_specs=(P(None, "chan", None), P("chan", None)),
        check_vma=False,
    )
```

time: 260 us -> 22.6 us (0.09); the launches traced: 256 us -> 22.3 us
  local copies, waits for them, and re-layouts: 161 us -> 4.26 us
  waiting for transfers between devices: 33.2 us -> 0 us
  blocking collectives: 20.6 us -> 0 us
  Pallas kernels: 0 us -> 17.4 us
  between operations: 14.5 us -> 0.66 us
  matrix products: 10.8 us -> 0 us
  other arithmetic: 9.23 us -> 0 us
  starting transfers between devices: 6.5 us -> 0 us
    gather x66 -> x0, local copies, waits for them, and re-layouts: 72.2 us -> none
    another operation x65 -> x0, local copies, waits for them, and re-layouts: 34.6 us -> none  [make_patches(): jnp.stack([padded[:, l:l + T_POS] for l in range(TL)], axis=-1)]
    psum x1 -> x0, waiting for transfers between devices: 32.7 us -> none  [body(): lax.psum((local_total * factor, numer * factor[None]), 'tmpl')]
    dot_general x1 -> x0, local copies, waits for them, and re-layouts: 24.7 us -> none  [block_scores(): lax.dot_general(flat, patches, (((1,), (1,)), ((), ())), preferred_elemen...]
    pallas_call x0 -> x1, Pallas kernels: none -> 17.4 us  [body(): pl.pallas_call(functools.partial(kernel, nchan, nz, count), out_shape=(ja...]
    reshape x1 -> x0, local copies, waits for them, and re-layouts: 15.1 us -> none  [block_scores(): plane = plane.reshape(count, TCH, rows_in, T_POS)]
    pmax x1 -> x0, blocking collectives: 12.1 us -> none  [body(): top = lax.pmax(local_top, 'tmpl')]
    dot_general x2 -> x0, matrix products: 10.8 us -> none  [the longest x1 10.4 us: block_scores(): lax.dot_general(flat, patches, (((1,), (1,)), ((), ())), preferred_elemen...]
  transfers between devices with their start and end apart: 3 -> 0, of which waited for: 2 -> 0; matrix products, arithmetic and copies ran while one was open for 1% -> 0% of each run, Pallas kernels for 0% -> 0%
where the time goes in v1:
time: 22.6 us; the launch traced here: 22.3 us
  Pallas kernels  17.4 us (77%)
  local copies, waits for them, and re-layouts  4.26 us (19%)
  between operations  0.66 us (3%)
    pallas_call x1, Pallas kernels, body(): pl.pallas_call(functools.partial(kernel, nchan, nz, count), out_shape=(ja...  17.4 us
    unnamed x12, local copies, waits for them, and re-layouts  4.26 us

profile of v1, /device:TPU:4, one launch (start us, length us, event | category | flops | bytes accessed | tf_op | source)
XLA Modules:
  0.0 22.3 jit_solution(13939556390890311841)
XLA Ops:
  0.6 0.0 copy-start.3
  0.6 0.0 copy-start.4
  0.7 0.6 %copy-done.3 = s32[64]{0:T(128)S(1)} copy-done((s32[64]{0:T(128)S(1)}, s32[64]{0:T(128)}, u32[]{:S(2)}) %copy-start.3) | copy-done | bytes 280
  1.3 0.0 copy-done.4
  1.3 0.0 copy-start
  1.3 0.9 %copy-done = bf16[64,16,128]{2,1,0:T(8,128)(2,1)S(1)} copy-done((bf16[64,16,128]{2,1,0:T(8,128)(2,1)S(1)}, bf16[64,16,128]{2,1,0:T(8,128)(2,1)}, u32[]{:S(2)}) %copy-start) | copy-done | bytes 262168
  2.3 0.0 copy-start.1
  2.3 0.7 %copy-done.1 = bf16[16,384]{1,0:T(8,128)(2,1)S(1)} copy-done((bf16[16,384]{1,0:T(8,128)(2,1)S(1)}, bf16[16,384]{1,0:T(8,128)(2,1)}, u32[]{:S(2)}) %copy-start.1) | copy-done | bytes 12312
  3.0 0.0 copy-start.2
  3.0 0.7 %copy-done.2 = f32[64,16]{0,1:T(8,128)S(1)} copy-done((f32[64,16]{0,1:T(8,128)S(1)}, f32[64,16]{0,1:T(8,128)}, u32[]{:S(2)}) %copy-start.2) | copy-done | bytes 4120
  3.7 17.4 %shard_map.68 = (f32[256,128]{1,0:T(8,128)S(1)}, f32[16,128]{1,0:T(8,128)S(1)}) custom-call(bf16[16,384]{1,0:T(8,128)(2,1)S(1)} %copy-done.1, bf16[1024,128]{1,0:T(8,128)(2,1)S(1)} %bitcast.5, s32[1,64]{1,0:T(1,128)S(1)} %bitcast.8, s32[1,16]{1,0:T(1,128)S(1)} %bitcast.9, f32[16,64]{1,0:T(8,128)S(1)} %bitcast.7), custom_call_target="tpu_custom_call" | custom-call | tf_op jit(solution)/shard_map/pallas_call | solution.py:267
  21.1 0.7 %copy.9 = f32[16,16,128]{2,1,0:T(8,128)} copy(f32[16,16,128]{2,1,0:T(8,128)S(1)} %bitcast.6) | data formatting | bytes 262144
  21.7 0.6 %copy.10 = f32[16,128]{1,0:T(8,128)} copy(f32[16,128]{1,0:T(8,128)S(1)} %get-tuple-element.9) | data formatting | bytes 16384
Async XLA Ops:
  0.6 0.7 %copy-start.3 = (s32[64]{0:T(128)S(1)}, s32[64]{0:T(128)}, u32[]{:S(2)}) copy-start(s32[64]{0:T(128)} %param.7) | copy-start | bytes 772
  0.6 0.7 %copy-start.4 = (s32[16]{0:T(128)S(1)}, s32[16]{0:T(128)}, u32[]{:S(2)}) copy-start(s32[16]{0:T(128)} %param.8) | copy-start | bytes 196
  1.3 0.9 %copy-start = (bf16[64,16,128]{2,1,0:T(8,128)(2,1)S(1)}, bf16[64,16,128]{2,1,0:T(8,128)(2,1)}, u32[]{:S(2)}) copy-start(bf16[64,16,128]{2,1,0:T(8,128)(2,1)} %param.6) | copy-start | bytes 786436
  2.3 0.7 %copy-start.1 = (bf16[16,384]{1,0:T(8,128)(2,1)S(1)}, bf16[16,384]{1,0:T(8,128)(2,1)}, u32[]{:S(2)}) copy-start(bf16[16,384]{1,0:T(8,128)(2,1)} %samples_ref.1) | copy-start | bytes 36868
  3.0 0.7 %copy-start.2 = (f32[64,16]{0,1:T(8,128)S(1)}, f32[64,16]{0,1:T(8,128)}, u32[]{:S(2)}) copy-start(f32[64,16]{0,1:T(8,128)} %param.9) | copy-start | bytes 12292

commit v2 on v1

--- a/solution.py
+++ b/solution.py
@@ -15,6 +15,9 @@
 WIN = 2 * REACH
 GROUP = 8
 STEPS = 40
+PARAM_MAX = 4.0
+VMEM_BYTES = 60 * 1024 * 1024
+CODE_MAX = 32767.0
 MESH = pl.DeviceIdType.MESH
 F32, BF16 = jnp.float32, jnp.bfloat16
 
@@ -74,12 +77,28 @@
         h2[low - 8 : first + n - 8, 8 * a : 8 * a + 16, 128:] = tile[low - first :]
 
 
+def encode(x):
+    m = jnp.clip(jnp.abs(x) * (1.0 / PARAM_MAX), 1e-30, 1.0)
+    y = jnp.exp2(0.125 * jnp.log2(m)) * CODE_MAX
+    return jnp.round(jnp.where(x < 0, -y, y)).astype(jnp.int16)
+
+
+def decode(code):
+    f = code.astype(F32)
+    y = jnp.abs(f) * (1.0 / CODE_MAX)
+    y = y * y
+    y = y * y
+    y = y * y * PARAM_MAX
+    return jnp.where(f < 0, -y, y)
+
+
 def kernel(
     nchan, nz, count,
+    samples_hbm, tmpl_hbm, start_hbm, shift_hbm, params_hbm,
+    gath, gev,
     samples_ref, tmpl_ref, start_ref, shift_ref, params_ref,
-    out_ref, ev_ref,
-    al, halo, tf, wp, e, h2, comb, recv, gath,
-    halo_send, halo_recv, rs_send, rs_recv, ag_send, ag_recv,
+    al, halo, tf, wp, e, h2, comb, cev, recv, rev, fin, fev,
+    in_sem, keep_sem, halo_send, halo_recv, rs_send, rs_recv, ag_send, ag_recv,
 ):
     cx, me = lax.axis_index("chan"), lax.axis_index("tmpl")
     q = 16 // nz
@@ -100,6 +119,23 @@
             barrier, inc=1, device_id={"tmpl": lax.rem(me + d, nz)}, device_id_type=MESH
         )
 
+    loads = [
+        pltpu.make_async_copy(src, dst, in_sem.at[i])
+        for i, (src, dst) in enumerate(
+            (
+                (shift_hbm, shift_ref),
+                (samples_hbm, samples_ref),
+                (start_hbm, start_ref),
+                (tmpl_hbm, tmpl_ref),
+                (params_hbm, params_ref),
+            )
+        )
+    ]
+    for load in loads:
+        load.start()
+
+    loads[0].wait()
+    loads[1].wait()
     x = samples_ref[...].astype(F32)
     shift = column(shift_ref[...], 16)
     for bit in (1, 2, 4, 8, 16, 32, 64, 128):
@@ -130,6 +166,9 @@
     def _():
         to_right().start()
 
+    loads[2].wait()
+    loads[3].wait()
+    loads[4].wait()
     build_filters(count, tmpl_ref, start_ref, tf, wp)
     build_hankel(mine, 16, e, h2)
 
@@ -164,13 +203,16 @@
     )
     scores = jnp.dot(lhs, h2[...].reshape(STEPS * TL, 256), preferred_element_type=F32)
 
-    comb[:, q * 16 :, :] = jnp.zeros((nz, 8, 128), F32)
+    cev[...] = jnp.zeros((nz, 8, 128), F32)
 
     def to_owner(z):
         slot = lax.rem(z - me + nz, nz)
-        return pltpu.make_async_remote_copy(
-            src_ref=comb.at[z], dst_ref=recv.at[slot], send_sem=rs_send.at[z],
-            recv_sem=rs_recv.at[slot], device_id={"tmpl": z}, device_id_type=MESH)
+        return [
+            pltpu.make_async_remote_copy(
+                src_ref=src.at[z], dst_ref=dst.at[slot], send_sem=rs_send.at[n, z],
+                recv_sem=rs_recv.at[n, slot], device_id={"tmpl": z}, device_id_type=MESH)
+            for n, (src, dst) in enumerate(((cev, rev), (comb, recv)))
+        ]
 
     for g in range(GROUP):
         s = scores[g * count : (g + 1) * count]
@@ -184,75 +226,112 @@
             + jnp.dot(pt_lo, w_hi, preferred_element_type=F32)
         )
         total = res[PARAMS : PARAMS + 1]
-        post = res[:PARAMS] / total
+        code = encode(res[:PARAMS] / total)
         ev = top + jnp.log(total)
         for half in range(2):
             i = 2 * g + half
             z, at = i // q, i % q
-            comb[z, at * 16 : at * 16 + 16, :] = post[:, half * 128 : half * 128 + 128]
-            comb[z, q * 16 + at : q * 16 + at + 1, :] = ev[:, half * 128 : half * 128 + 128]
+            comb[z, at * 16 : at * 16 + 16, :] = code[:, half * 128 : half * 128 + 128]
+            cev[z, at : at + 1, :] = ev[:, half * 128 : half * 128 + 128]
             if at == q - 1:
 
                 @pl.when(me != z)
                 def _():
-                    to_owner(z).start()
+                    for copy in to_owner(z):
+                        copy.start()
 
     for d in range(1, nz):
-        pltpu.make_async_remote_copy(
-            src_ref=comb.at[d], dst_ref=recv.at[d], send_sem=rs_send.at[d],
-            recv_sem=rs_recv.at[d], device_id={"tmpl": lax.rem(me + d, nz)}, device_id_type=MESH
-        ).wait_recv()
-
-    evs = [comb[me, q * 16 :, :]] + [recv[d, q * 16 :, :] for d in range(1, nz)]
+        for n, (src, dst) in enumerate(((cev, rev), (comb, recv))):
+            pltpu.make_async_remote_copy(
+                src_ref=src.at[d], dst_ref=dst.at[d], send_sem=rs_send.at[n, d],
+                recv_sem=rs_recv.at[n, d], device_id={"tmpl": lax.rem(me + d, nz)},
+                device_id_type=MESH).wait_recv()
+
+    evs = [cev[me]] + [rev[d] for d in range(1, nz)]
     top = functools.reduce(jnp.maximum, evs)
     parts = [jnp.exp(v - top) for v in evs]
     total = functools.reduce(jnp.add, parts)
-    gath[me, q * 16 :, :] = top + jnp.log(total)
+    fev[...] = top + jnp.log(total)
     inv = 1.0 / total
     shares = [v * inv for v in parts]
     for at in range(q):
         rows = slice(at * 16, at * 16 + 16)
-        acc = shares[0][at : at + 1] * comb[me, rows, :]
+        acc = shares[0][at : at + 1] * decode(comb[me, rows, :])
         for d in range(1, nz):
-            acc = acc + shares[d][at : at + 1] * recv[d, rows, :]
-        gath[me, rows, :] = acc
+            acc = acc + shares[d][at : at + 1] * decode(recv[d, rows, :])
+        fin[rows, :] = encode(acc)
 
     def to_peer(d):
-        return pltpu.make_async_remote_copy(
-            src_ref=gath.at[me], dst_ref=gath.at[me], send_sem=ag_send.at[d],
-            recv_sem=ag_recv.at[me], device_id={"tmpl": lax.rem(me + d, nz)}, device_id_type=MESH)
+        return [
+            pltpu.make_async_remote_copy(
+                src_ref=src, dst_ref=ref.at[me], send_sem=ag_send.at[n, d],
+                recv_sem=ag_recv.at[n, me], device_id={"tmpl": lax.rem(me + d, nz)},
+                device_id_type=MESH)
+            for n, (src, ref) in enumerate(((fev, gev), (fin, gath)))
+        ]
 
     for d in range(1, nz):
-        to_peer(d).start()
+        for copy in to_peer(d):
+            copy.start()
+    keeps = [
+        pltpu.make_async_copy(fev, gev.at[me], keep_sem.at[0]),
+        pltpu.make_async_copy(fin, gath.at[me], keep_sem.at[1]),
+    ]
+    for keep in keeps:
+        keep.start()
     for d in range(1, nz):
         z = lax.rem(me + d, nz)
-        pltpu.make_async_remote_copy(
-            src_ref=gath.at[z], dst_ref=gath.at[z], send_sem=ag_send.at[d],
-            recv_sem=ag_recv.at[z], device_id={"tmpl": z}, device_id_type=MESH
-        ).wait_recv()
-
+        for n, (src, ref) in enumerate(((fev, gev), (fin, gath))):
+            pltpu.make_async_remote_copy(
+                src_ref=src, dst_ref=ref.at[z], send_sem=ag_send.at[n, d],
+                recv_sem=ag_recv.at[n, z], device_id={"tmpl": z}, device_id_type=MESH
+            ).wait_recv()
+    for keep in keeps:
+        keep.wait()
+
+    @pl.when(has_left)
+    def _():
+        to_left().wait_send()
+
+    @pl.when(has_right)
+    def _():
+        to_right().wait_send()
+
+    for z in range(nz):
+
+        @pl.when(me != z)
+        def _():
+            for copy in to_owner(z):
+                copy.wait_send()
+
+    for d in range(1, nz):
+        for copy in to_peer(d):
+            copy.wait_send()
+
+
+def unpack(nz, gath_hbm, gev_hbm, out_hbm, ev_hbm, gath, gev, out_ref, ev_ref, in_sem, sem):
+    q = 16 // nz
+    load = pltpu.make_async_copy(gev_hbm, gev, in_sem.at[nz])
+    loads = [pltpu.make_async_copy(gath_hbm.at[z], gath.at[z], in_sem.at[z]) for z in range(nz)]
+    load.start()
+    for copy in loads:
+        copy.start()
+    load.wait()
     for i in range(16):
+        if i % q == 0:
+            loads[i // q].wait()
         c = 8 * (i % 2) + i // 2
         z, at = i // q, i % q
-        out_ref[pl.ds(c, PARAMS, stride=16), :] = gath[z, at * 16 : at * 16 + 16, :]
-        ev_ref[c : c + 1, :] = gath[z, q * 16 + at : q * 16 + at + 1, :]
-
-    @pl.when(has_left)
-    def _():
-        to_left().wait_send()
-
-    @pl.when(has_right)
-    def _():
-        to_right().wait_send()
-
-    for z in range(nz):
-
-        @pl.when(me != z)
-        def _():
-            to_owner(z).wait_send()
-
-    for d in range(1, nz):
-        to_peer(d).wait_send()
+        ev_ref[c : c + 1, :] = gev[z, at : at + 1, :]
+        out_ref[pl.ds(c, PARAMS, stride=16), :] = decode(gath[z, at * 16 : at * 16 + 16, :])
+    copies = [
+        pltpu.make_async_copy(ev_ref, ev_hbm, sem.at[0]),
+        pltpu.make_async_copy(out_ref, out_hbm, sem.at[1]),
+    ]
+    for copy in copies:
+        copy.start()
+    for copy in copies:
+        copy.wait()
 
 
 def solution(mesh):
@@ -261,36 +340,45 @@
     def body(samples, templates, start_chan, chan_shift, params):
         rows, count = samples.shape[0], templates.shape[0]
         assert rows == 16 and 16 % nz == 0
-        piece = 16 // nz * 16 + 8
-        vmem = pl.BlockSpec(memory_space=pltpu.VMEM)
+        piece = 16 // nz * 16
+        hbm = pl.BlockSpec(memory_space=pltpu.HBM)
         dma = pltpu.SemaphoreType.DMA
-        post, ev = pl.pallas_call(
+        codes = pltpu.VMEM((nz, piece, 128), jnp.int16)
+        evs = pltpu.VMEM((nz, 8, 128), F32)
+        gath, gev = pl.pallas_call(
             functools.partial(kernel, nchan, nz, count),
             out_shape=(
-                jax.ShapeDtypeStruct((PARAMS * rows, T_POS), F32),
-                jax.ShapeDtypeStruct((rows, T_POS), F32),
+                jax.ShapeDtypeStruct((nz, piece, 128), jnp.int16),
+                jax.ShapeDtypeStruct((nz, 8, 128), F32),
             ),
-            in_specs=[vmem] * 5,
-            out_specs=(vmem, vmem),
+            in_specs=[hbm] * 5,
+            out_specs=(hbm, hbm),
             scratch_shapes=[
+                pltpu.VMEM(samples.shape, BF16),
+                pltpu.VMEM((count * TCH, TL), BF16),
+                pltpu.VMEM((1, count), jnp.int32),
+                pltpu.VMEM((1, rows), jnp.int32),
+                pltpu.VMEM((PARAMS, count), F32),
                 pltpu.VMEM((16, 256), BF16),
                 pltpu.VMEM((2, 16, 256), BF16),
                 pltpu.VMEM((count * TCH, TL), F32),
                 pltpu.VMEM((count, (2 * GROUP - 1 + WIN) * TL), BF16),
                 pltpu.VMEM((2 * 48 * 8, 128), F32),
                 pltpu.VMEM((STEPS, TL, 256), BF16),
-                pltpu.VMEM((nz, piece, 128), F32),
-                pltpu.VMEM((nz, piece, 128), F32),
-                pltpu.VMEM((nz, piece, 128), F32),
+                codes, evs, codes, evs,
+                pltpu.VMEM((piece, 128), jnp.int16),
+                pltpu.VMEM((8, 128), F32),
+                dma((5,)),
                 dma((2,)),
                 dma((2,)),
-                dma((nz,)),
-                dma((nz,)),
-                dma((nz,)),
-                dma((nz,)),
+                dma((2,)),
+                dma((2, nz)),
+                dma((2, nz)),
+                dma((2, nz)),
+                dma((2, nz)),
             ],
             compiler_params=pltpu.CompilerParams(
-                collective_id=0, has_side_effects=True, vmem_limit_bytes=40 * 1024 * 1024
+                collective_id=0, has_side_effects=True, vmem_limit_bytes=VMEM_BYTES
             ),
         )(
             samples,
@@ -299,6 +387,23 @@
             chan_shift.reshape(1, rows),
             params.T,
         )
+        post, ev = pl.pallas_call(
+            functools.partial(unpack, nz),
+            out_shape=(
+                jax.ShapeDtypeStruct((PARAMS * rows, T_POS), F32),
+                jax.ShapeDtypeStruct((rows, T_POS), F32),
+            ),
+            in_specs=[hbm, hbm],
+            out_specs=(hbm, hbm),
+            scratch_shapes=[
+                codes, evs,
+                pltpu.VMEM((PARAMS * rows, T_POS), F32),
+                pltpu.VMEM((rows, T_POS), F32),
+                dma((nz + 1,)),
+                dma((2,)),
+            ],
+            compiler_params=pltpu.CompilerParams(vmem_limit_bytes=VMEM_BYTES),
+        )(gath, gev)
         return post.reshape(PARAMS, rows, T_POS), ev
 
     placed = (P("chan", None), P("tmpl", None, None), P("tmpl"), P("chan"), P("tmpl", None))

time: 22.6 us -> 18.7 us (0.83)
  local copies, waits for them, and re-layouts: 4.26 us -> 0 us
  Pallas kernels: 17.4 us -> 17.8 us
    unnamed x12 -> x0, local copies, waits for them, and re-layouts: 4.26 us -> none
    pallas_call x0 -> x1, Pallas kernels: none -> 1.54 us  [body(): pl.pallas_call(functools.partial(unpack, nz), out_shape=(jax.ShapeDtypeSt...]
    pallas_call x1, Pallas kernels: 17.4 us -> 16.3 us  [body(): pl.pallas_call(functools.partial(kernel, nchan, nz, count), out_shape=(ja...]
where the time goes in v2:
time: 18.7 us; the launch traced here: 18.5 us
  Pallas kernels  17.8 us (95%)
  between operations  0.64 us (3%)
    pallas_call x1, Pallas kernels, body(): pl.pallas_call(functools.partial(kernel, nchan, nz, count), out_shape=(ja...  16.3 us
    pallas_call x1, Pallas kernels, body(): pl.pallas_call(functools.partial(unpack, nz), out_shape=(jax.ShapeDtypeSt...  1.54 us

profile of v2, /device:TPU:4, one launch (start us, length us, event | category | flops | bytes accessed | tf_op | source)
XLA Modules:
  0.0 18.5 jit_solution(16747408961468369040)
XLA Ops:
  0.6 16.3 %shard_map.68 = (s16[4,64,128]{2,1,0:T(8,128)(2,1)}, f32[4,8,128]{2,1,0:T(8,128)}) custom-call(bf16[16,384]{1,0:T(8,128)(2,1)} %samples_hbm.1, bf16[1024,128]{1,0:T(8,128)(2,1)} %bitcast.5, s32[1,64]{1,0:T(1,128)} %bitcast.7, s32[1,16]{1,0:T(1,128)} %bitcast.8, f32[16,64]{1,0:T(8,128)} %bitcast.6), custom_call_target="tpu_custom_call" | custom-call | tf_op jit(solution)/shard_map/pallas_call | solution.py:348
  16.9 1.5 %shard_map.69 = (f32[256,128]{1,0:T(8,128)}, f32[16,128]{1,0:T(8,128)}) custom-call(s16[4,64,128]{2,1,0:T(8,128)(2,1)} %get-tuple-element.6.gath_hbm, f32[4,8,128]{2,1,0:T(8,128)} %get-tuple-element.7.gev_hbm), custom_call_target="tpu_custom_call" | custom-call | tf_op jit(solution)/shard_map/pallas_call | solution.py:390

commit v3 on v2

--- a/solution.py
+++ b/solution.py
@@ -16,8 +16,10 @@
 GROUP = 8
 STEPS = 40
 PARAM_MAX = 4.0
-VMEM_BYTES = 60 * 1024 * 1024
+VMEM_BYTES = 40 * 1024 * 1024
 CODE_MAX = 32767.0
+EV_STEP = 8.0
+EV_FINE = 8191.0
 MESH = pl.DeviceIdType.MESH
 F32, BF16 = jnp.float32, jnp.bfloat16
 
@@ -92,13 +94,32 @@
     return jnp.where(f < 0, -y, y)
 
 
+def encode_evidence(ev):
+    coarse = jnp.round(ev * (1.0 / EV_STEP))
+    fine = jnp.round((ev - coarse * EV_STEP) * EV_FINE)
+    return jnp.concatenate([coarse, fine], axis=0).astype(jnp.int16)
+
+
+def decode_evidence(code):
+    f = code.astype(F32)
+    return f[:8] * EV_STEP + f[8:] * (1.0 / EV_FINE)
+
+
+def align(x, shift_row):
+    shift = column(shift_row, x.shape[0])
+    for bit in (1, 2, 4, 8, 16, 32, 64, 128):
+        on = (jnp.broadcast_to(shift, x.shape) & bit) != 0
+        x = jnp.where(on, pltpu.roll(x, x.shape[1] - bit, 1), x)
+    return x[:, : T_POS + TL]
+
+
 def kernel(
     nchan, nz, count,
     samples_hbm, tmpl_hbm, start_hbm, shift_hbm, params_hbm,
-    gath, gev,
+    gath,
     samples_ref, tmpl_ref, start_ref, shift_ref, params_ref,
-    al, halo, tf, wp, e, h2, comb, cev, recv, rev, fin, fev,
-    in_sem, keep_sem, halo_send, halo_recv, rs_send, rs_recv, ag_send, ag_recv,
+    al, halo, tf, wp, e, h2, comb, cev, recv,
+    in_sem, halo_send, halo_recv, rs_send, rs_recv, ag_send, ag_recv,
 ):
     cx, me = lax.axis_index("chan"), lax.axis_index("tmpl")
     q = 16 // nz
@@ -136,35 +157,34 @@
 
     loads[0].wait()
     loads[1].wait()
-    x = samples_ref[...].astype(F32)
-    shift = column(shift_ref[...], 16)
-    for bit in (1, 2, 4, 8, 16, 32, 64, 128):
-        on = (jnp.broadcast_to(shift, x.shape) & bit) != 0
-        x = jnp.where(on, pltpu.roll(x, x.shape[1] - bit, 1), x)
-    mine = x[:, : T_POS + TL]
+    mine = align(samples_ref[...].astype(F32), shift_ref[...])
     al[...] = mine.astype(BF16)
 
     pl.semaphore_wait(
         barrier, nz - 1 + has_left.astype(jnp.int32) + has_right.astype(jnp.int32)
     )
 
-    def to_left():
+    def to_side(side):
+        land = 1 - side
         return pltpu.make_async_remote_copy(
-            src_ref=al, dst_ref=halo.at[1], send_sem=halo_send.at[0], recv_sem=halo_recv.at[1],
-            device_id={"chan": cx - 1}, device_id_type=MESH)
-
-    def to_right():
-        return pltpu.make_async_remote_copy(
-            src_ref=al, dst_ref=halo.at[0], send_sem=halo_send.at[1], recv_sem=halo_recv.at[0],
-            device_id={"chan": cx + 1}, device_id_type=MESH)
-
-    @pl.when(has_left)
-    def _():
-        to_left().start()
-
-    @pl.when(has_right)
-    def _():
-        to_right().start()
+            src_ref=al, dst_ref=halo.at[land], send_sem=halo_send.at[side],
+            recv_sem=halo_recv.at[land], device_id={"chan": cx + 2 * side - 1},
+            device_id_type=MESH)
+
+    def send_side(side):
+        to_side(side).start()
+
+    def got_from(side):
+        to_side(1 - side).wait_recv()
+
+    def none_from(side):
+        halo[side] = jnp.zeros(halo.shape[1:], BF16)
+
+    def sent_side(side):
+        to_side(side).wait_send()
+
+    pl.when(has_left)(lambda: send_side(0))
+    pl.when(has_right)(lambda: send_side(1))
 
     loads[2].wait()
     loads[3].wait()
@@ -179,21 +199,10 @@
     pt_hi = jnp.concatenate([p_hi.astype(F32), below], axis=0).astype(BF16)
     pt_lo = jnp.concatenate([p_lo, jnp.zeros((16, count), F32)], axis=0).astype(BF16)
 
-    @pl.when(has_left)
-    def _():
-        to_right().wait_recv()
-
-    @pl.when(jnp.logical_not(has_left))
-    def _():
-        halo[0] = jnp.zeros((16, 256), BF16)
-
-    @pl.when(has_right)
-    def _():
-        to_left().wait_recv()
-
-    @pl.when(jnp.logical_not(has_right))
-    def _():
-        halo[1] = jnp.zeros((16, 256), BF16)
+    pl.when(has_left)(lambda: got_from(0))
+    pl.when(jnp.logical_not(has_left))(lambda: none_from(0))
+    pl.when(has_right)(lambda: got_from(1))
+    pl.when(jnp.logical_not(has_right))(lambda: none_from(1))
 
     build_hankel(halo[0].astype(F32), 0, e, h2)
     build_hankel(halo[1].astype(F32), 32, e, h2)
@@ -207,12 +216,9 @@
 
     def to_owner(z):
         slot = lax.rem(z - me + nz, nz)
-        return [
-            pltpu.make_async_remote_copy(
-                src_ref=src.at[z], dst_ref=dst.at[slot], send_sem=rs_send.at[n, z],
-                recv_sem=rs_recv.at[n, slot], device_id={"tmpl": z}, device_id_type=MESH)
-            for n, (src, dst) in enumerate(((cev, rev), (comb, recv)))
-        ]
+        return pltpu.make_async_remote_copy(
+            src_ref=comb.at[z], dst_ref=recv.at[slot], send_sem=rs_send.at[z],
+            recv_sem=rs_recv.at[slot], device_id={"tmpl": z}, device_id_type=MESH)
 
     for g in range(GROUP):
         s = scores[g * count : (g + 1) * count]
@@ -234,24 +240,23 @@
             comb[z, at * 16 : at * 16 + 16, :] = code[:, half * 128 : half * 128 + 128]
             cev[z, at : at + 1, :] = ev[:, half * 128 : half * 128 + 128]
             if at == q - 1:
+                comb[z, q * 16 :, :] = encode_evidence(cev[z])
 
                 @pl.when(me != z)
                 def _():
-                    for copy in to_owner(z):
-                        copy.start()
-
-    for d in range(1, nz):
-        for n, (src, dst) in enumerate(((cev, rev), (comb, recv))):
-            pltpu.make_async_remote_copy(
-                src_ref=src.at[d], dst_ref=dst.at[d], send_sem=rs_send.at[n, d],
-                recv_sem=rs_recv.at[n, d], device_id={"tmpl": lax.rem(me + d, nz)},
-                device_id_type=MESH).wait_recv()
-
-    evs = [cev[me]] + [rev[d] for d in range(1, nz)]
+                    to_owner(z).start()
+
+    for d in range(1, nz):
+        pltpu.make_async_remote_copy(
+            src_ref=comb.at[d], dst_ref=recv.at[d], send_sem=rs_send.at[d],
+            recv_sem=rs_recv.at[d], device_id={"tmpl": lax.rem(me + d, nz)},
+            device_id_type=MESH).wait_recv()
+
+    evs = [cev[me]] + [decode_evidence(recv[d, q * 16 :, :]) for d in range(1, nz)]
     top = functools.reduce(jnp.maximum, evs)
     parts = [jnp.exp(v - top) for v in evs]
     total = functools.reduce(jnp.add, parts)
-    fev[...] = top + jnp.log(total)
+    gath[me, q * 16 :, :] = encode_evidence(top + jnp.log(total))
     inv = 1.0 / total
     shares = [v * inv for v in parts]
     for at in range(q):
@@ -259,71 +264,42 @@
         acc = shares[0][at : at + 1] * decode(comb[me, rows, :])
         for d in range(1, nz):
             acc = acc + shares[d][at : at + 1] * decode(recv[d, rows, :])
-        fin[rows, :] = encode(acc)
+        gath[me, rows, :] = encode(acc)
 
     def to_peer(d):
-        return [
-            pltpu.make_async_remote_copy(
-                src_ref=src, dst_ref=ref.at[me], send_sem=ag_send.at[n, d],
-                recv_sem=ag_recv.at[n, me], device_id={"tmpl": lax.rem(me + d, nz)},
-                device_id_type=MESH)
-            for n, (src, ref) in enumerate(((fev, gev), (fin, gath)))
-        ]
-
-    for d in range(1, nz):
-        for copy in to_peer(d):
-            copy.start()
-    keeps = [
-        pltpu.make_async_copy(fev, gev.at[me], keep_sem.at[0]),
-        pltpu.make_async_copy(fin, gath.at[me], keep_sem.at[1]),
-    ]
-    for keep in keeps:
-        keep.start()
-    for d in range(1, nz):
-        z = lax.rem(me + d, nz)
-        for n, (src, ref) in enumerate(((fev, gev), (fin, gath))):
-            pltpu.make_async_remote_copy(
-                src_ref=src, dst_ref=ref.at[z], send_sem=ag_send.at[n, d],
-                recv_sem=ag_recv.at[n, z], device_id={"tmpl": z}, device_id_type=MESH
-            ).wait_recv()
-    for keep in keeps:
-        keep.wait()
-
-    @pl.when(has_left)
-    def _():
-        to_left().wait_send()
-
-    @pl.when(has_right)
-    def _():
-        to_right().wait_send()
-
+        return pltpu.make_async_remote_copy(
+            src_ref=gath.at[me], dst_ref=gath.at[me], send_sem=ag_send.at[d],
+            recv_sem=ag_recv.at[me], device_id={"tmpl": lax.rem(me + d, nz)}, device_id_type=MESH)
+
+    for d in range(1, nz):
+        to_peer(d).start()
+
+    pl.when(has_left)(lambda: sent_side(0))
+    pl.when(has_right)(lambda: sent_side(1))
     for z in range(nz):
 
         @pl.when(me != z)
         def _():
-            for copy in to_owner(z):
-                copy.wait_send()
-
-    for d in range(1, nz):
-        for copy in to_peer(d):
-            copy.wait_send()
-
-
-def unpack(nz, gath_hbm, gev_hbm, out_hbm, ev_hbm, gath, gev, out_ref, ev_ref, in_sem, sem):
+            to_owner(z).wait_send()
+
+    for d in range(1, nz):
+        z = lax.rem(me + d, nz)
+        pltpu.make_async_remote_copy(
+            src_ref=gath.at[z], dst_ref=gath.at[z], send_sem=ag_send.at[d],
+            recv_sem=ag_recv.at[z], device_id={"tmpl": z}, device_id_type=MESH).wait_recv()
+    for d in range(1, nz):
+        to_peer(d).wait_send()
+
+
+def unpack(nz, gath, out_hbm, ev_hbm, out_ref, ev_ref, sem):
     q = 16 // nz
-    load = pltpu.make_async_copy(gev_hbm, gev, in_sem.at[nz])
-    loads = [pltpu.make_async_copy(gath_hbm.at[z], gath.at[z], in_sem.at[z]) for z in range(nz)]
-    load.start()
-    for copy in loads:
-        copy.start()
-    load.wait()
-    for i in range(16):
-        if i % q == 0:
-            loads[i // q].wait()
-        c = 8 * (i % 2) + i // 2
-        z, at = i // q, i % q
-        ev_ref[c : c + 1, :] = gev[z, at : at + 1, :]
-        out_ref[pl.ds(c, PARAMS, stride=16), :] = decode(gath[z, at * 16 : at * 16 + 16, :])
+    for z in range(nz):
+        ev = decode_evidence(gath[z, q * 16 :, :])
+        for at in range(q):
+            i = z * q + at
+            c = 8 * (i % 2) + i // 2
+            ev_ref[c : c + 1, :] = ev[at : at + 1]
+            out_ref[pl.ds(c, PARAMS, stride=16), :] = decode(gath[z, at * 16 : at * 16 + 16, :])
     copies = [
         pltpu.make_async_copy(ev_ref, ev_hbm, sem.at[0]),
         pltpu.make_async_copy(out_ref, out_hbm, sem.at[1]),
@@ -340,19 +316,17 @@
     def body(samples, templates, start_chan, chan_shift, params):
         rows, count = samples.shape[0], templates.shape[0]
         assert rows == 16 and 16 % nz == 0
-        piece = 16 // nz * 16
+        piece = 16 // nz * 16 + 16
+        vmem = pl.BlockSpec(memory_space=pltpu.VMEM)
         hbm = pl.BlockSpec(memory_space=pltpu.HBM)
         dma = pltpu.SemaphoreType.DMA
         codes = pltpu.VMEM((nz, piece, 128), jnp.int16)
         evs = pltpu.VMEM((nz, 8, 128), F32)
-        gath, gev = pl.pallas_call(
+        gath = pl.pallas_call(
             functools.partial(kernel, nchan, nz, count),
-            out_shape=(
-                jax.ShapeDtypeStruct((nz, piece, 128), jnp.int16),
-                jax.ShapeDtypeStruct((nz, 8, 128), F32),
-            ),
+            out_shape=pltpu.VMEM((nz, piece, 128), jnp.int16),
             in_specs=[hbm] * 5,
-            out_specs=(hbm, hbm),
+            out_specs=vmem,
             scratch_shapes=[
                 pltpu.VMEM(samples.shape, BF16),
                 pltpu.VMEM((count * TCH, TL), BF16),
@@ -365,27 +339,29 @@
                 pltpu.VMEM((count, (2 * GROUP - 1 + WIN) * TL), BF16),
                 pltpu.VMEM((2 * 48 * 8, 128), F32),
                 pltpu.VMEM((STEPS, TL, 256), BF16),
-                codes, evs, codes, evs,
-                pltpu.VMEM((piece, 128), jnp.int16),
-                pltpu.VMEM((8, 128), F32),
+                codes, evs, codes,
                 dma((5,)),
                 dma((2,)),
                 dma((2,)),
-                dma((2,)),
-                dma((2, nz)),
-                dma((2, nz)),
-                dma((2, nz)),
-                dma((2, nz)),
+                dma((nz,)),
+                dma((nz,)),
+                dma((nz,)),
+                dma((nz,)),
             ],
             compiler_params=pltpu.CompilerParams(
                 collective_id=0, has_side_effects=True, vmem_limit_bytes=VMEM_BYTES
             ),
         )(
-            samples,
-            templates.reshape(count * TCH, TL),
-            start_chan.reshape(1, count),
-            chan_shift.reshape(1, rows),
-            params.T,
+            *(
+                pltpu.with_memory_space_constraint(v, pltpu.HBM)
+                for v in (
+                    samples,
+                    templates.reshape(count * TCH, TL),
+                    start_chan.reshape(1, count),
+                    chan_shift.reshape(1, rows),
+                    params.T,
+                )
+            )
         )
         post, ev = pl.pallas_call(
             functools.partial(unpack, nz),
@@ -393,17 +369,15 @@
                 jax.ShapeDtypeStruct((PARAMS * rows, T_POS), F32),
                 jax.ShapeDtypeStruct((rows, T_POS), F32),
             ),
-            in_specs=[hbm, hbm],
+            in_specs=[vmem],
             out_specs=(hbm, hbm),
             scratch_shapes=[
-                codes, evs,
                 pltpu.VMEM((PARAMS * rows, T_POS), F32),
                 pltpu.VMEM((rows, T_POS), F32),
-                dma((nz + 1,)),
                 dma((2,)),
             ],
             compiler_params=pltpu.CompilerParams(vmem_limit_bytes=VMEM_BYTES),
-        )(gath, gev)
+        )(gath)
         return post.reshape(PARAMS, rows, T_POS), ev
 
     placed = (P("chan", None), P("tmpl", None, None), P("tmpl"), P("chan"), P("tmpl", None))

time: 18.7 us -> 17.6 us (0.941)
  Pallas kernels: 17.8 us -> 16.8 us
    pallas_call x1, Pallas kernels: 1.54 us -> 0.75 us  [body(): pl.pallas_call(functools.partial(unpack, nz), out_shape=(jax.ShapeDtypeSt...]
    pallas_call x1, Pallas kernels: 16.3 us -> 16 us  [body(): pl.pallas_call(functools.partial(kernel, nchan, nz, count), out_shape=plt...]
where the time goes in v3:
time: 17.6 us; the launch traced here: 17.4 us
  Pallas kernels  16.8 us (95%)
  between operations  0.64 us (4%)
    pallas_call x1, Pallas kernels, body(): pl.pallas_call(functools.partial(kernel, nchan, nz, count), out_shape=plt...  16 us
    pallas_call x1, Pallas kernels, body(): pl.pallas_call(functools.partial(unpack, nz), out_shape=(jax.ShapeDtypeSt...  0.75 us

profile of v3, /device:TPU:4, one launch (start us, length us, event | category | flops | bytes accessed | tf_op | source)
XLA Modules:
  0.0 17.4 jit_solution(18411644028958712229)
XLA Ops:
  0.6 16.0 %shard_map.68.gath = s16[4,80,128]{2,1,0:T(8,128)(2,1)S(1)} custom-call(bf16[16,384]{1,0:T(8,128)(2,1)} %samples_hbm.1, bf16[1024,128]{1,0:T(8,128)(2,1)} %bitcast.5, s32[1,64]{1,0:T(1,128)} %bitcast.7, s32[1,16]{1,0:T(1,128)} %bitcast.8, f32[16,64]{1,0:T(8,128)} %bitcast.6), custom_call_target="tpu_custom_call" | custom-call | tf_op jit(solution)/shard_map/pallas_call | solution.py:325
  16.7 0.8 %shard_map.69 = (f32[256,128]{1,0:T(8,128)}, f32[16,128]{1,0:T(8,128)}) custom-call(s16[4,80,128]{2,1,0:T(8,128)(2,1)S(1)} %shard_map.68.gath), custom_call_target="tpu_custom_call" | custom-call | tf_op jit(solution)/shard_map/pallas_call | solution.py:366

commit v4 on v3

--- a/solution.py
+++ b/solution.py
@@ -201,10 +201,10 @@
 
     pl.when(has_left)(lambda: got_from(0))
     pl.when(jnp.logical_not(has_left))(lambda: none_from(0))
+
+    build_hankel(halo[0].astype(F32), 0, e, h2)
     pl.when(has_right)(lambda: got_from(1))
     pl.when(jnp.logical_not(has_right))(lambda: none_from(1))
-
-    build_hankel(halo[0].astype(F32), 0, e, h2)
     build_hankel(halo[1].astype(F32), 32, e, h2)
 
     lhs = jnp.concatenate(

time: 17.6 us -> 18 us (1.023)
  Pallas kernels: 16.8 us -> 17.2 us
    pallas_call x1, Pallas kernels: 16 us -> 16.5 us  [body(): pl.pallas_call(functools.partial(kernel, nchan, nz, count), out_shape=plt...]
where the time goes in v4:
time: 18 us; the launch traced here: 17.9 us
  Pallas kernels  17.2 us (96%)
  between operations  0.64 us (4%)
    pallas_call x1, Pallas kernels, body(): pl.pallas_call(functools.partial(kernel, nchan, nz, count), out_shape=plt...  16.5 us
    pallas_call x1, Pallas kernels, body(): pl.pallas_call(functools.partial(unpack, nz), out_shape=(jax.ShapeDtypeSt...  0.75 us

profile of v4, /device:TPU:4, one launch (start us, length us, event | category | flops | bytes accessed | tf_op | source)
XLA Modules:
  0.0 17.9 jit_solution(5845855509259953231)
XLA Ops:
  0.6 16.5 %shard_map.68.gath = s16[4,80,128]{2,1,0:T(8,128)(2,1)S(1)} custom-call(bf16[16,384]{1,0:T(8,128)(2,1)} %samples_hbm.1, bf16[1024,128]{1,0:T(8,128)(2,1)} %bitcast.5, s32[1,64]{1,0:T(1,128)} %bitcast.7, s32[1,16]{1,0:T(1,128)} %bitcast.8, f32[16,64]{1,0:T(8,128)} %bitcast.6), custom_call_target="tpu_custom_call" | custom-call | tf_op jit(solution)/shard_map/pallas_call | solution.py:325
  17.1 0.8 %shard_map.69 = (f32[256,128]{1,0:T(8,128)}, f32[16,128]{1,0:T(8,128)}) custom-call(s16[4,80,128]{2,1,0:T(8,128)(2,1)S(1)} %shard_map.68.gath), custom_call_target="tpu_custom_call" | custom-call | tf_op jit(solution)/shard_map/pallas_call | solution.py:366
